TPU v7x, 32 devices: a whole 2x2x4 slice. The times are simulated.
32 devices in a mesh: ens: 2 (over x), tm: 16 (over z, y, core).
Axes of the slice: x: 2, y: 2, z: 4, core: 2. Of those that a mesh axis runs over, the one named last changes fastest.
Arguments:
- observed: float32 [32, 3000], P(('ens', 'tm')), parts along dimension 0, may hold values from -6 to 6
- present: int32 [32, 3000], P(('ens', 'tm')), parts along dimension 0, may hold values 0 or 1
- loading: float32 [3000, 16], replicated, may hold values from -1.5 to 1.5
- noise_var: float32 [3000], replicated, may hold values from 0.25 to 1
- region_block: int32 [3000], replicated, may hold values from 0 to 127
- transition: float32 [16, 16, 128], replicated, may hold values from -1 to 1
- innovation: float32 [2048], replicated, may hold values from 0.05 to 0.5
- prior_mean: float32 [2048], replicated, may hold values from -4 to 4
- prior_var: float32 [2048], replicated, may hold values from 0.5 to 2
Outputs:
- filtered_mean: float32 [32, 2048], P(('ens', 'tm')), parts along dimension 0
- smoothed_mean: float32 [32, 2048], P(('ens', 'tm')), parts along dimension 0
- smoothed_var: float32 [32, 2048], P(('ens', 'tm')), parts along dimension 0
There are 2 independent parts, one for each index of `ens`. A program takes and returns all parts, laid end to end along the dimension named above; an argument that names none is the same for every part. Nothing has to cross between parts.
All inputs are finite; a program needn't handle non-finite values. No bound on the sum of `present` on one device may be relied on, other than what follows from the above.
Results may differ from a plain program's by a relative error of at most 0.0003.
Values sent between devices are 32-bit elements; how exact they have to be, the bound alone decides.
A program may use at most 128 MiB of HBM per device.

v0:
```python
import functools
import jax
import jax.numpy as jnp
from jax import lax
from jax.experimental import pallas as pl
from jax.experimental.pallas import tpu as pltpu
from jax.sharding import PartitionSpec as P

MESH = pl.DeviceIdType.MESH
W = 16
W2 = W * W
LANES = 128
CHUNK = 512


def negative_inverse(rows):
    sub = lax.broadcasted_iota(jnp.int32, (W, LANES), 0)
    rows = list(rows)
    for p in range(W):
        row = rows[p]
        d = 1.0 / row[p : p + 1, :]
        here = sub == p
        scaled = jnp.where(here, -d, row * d)
        for i in range(W):
            if i == p:
                rows[i] = scaled
            else:
                rows[i] = jnp.where(here, 0.0, rows[i]) - row[i : i + 1, :] * scaled
    return rows


def store_rows(ref, rows):
    for i in range(W):
        ref[i * W : (i + 1) * W, :] = rows[i]


def load_rows(ref):
    return [ref[i * W : (i + 1) * W, :] for i in range(W)]


def load_columns(ref):
    return [ref[pl.ds(k, W, stride=W), :] for k in range(W)]


def multiply(out_ref, left_ref, right_rows, turned=False, start=None, mask=None):
    def one(i, carry):
        at = pl.multiple_of(i * W, W)
        total = None
        for k in range(W):
            row = k * W + i if turned else i * W + k
            term = left_ref[pl.ds(row, 1), :] * right_rows[k]
            total = term if total is None else total + term
        if start is not None:
            total = total + start[pl.ds(at, W), :]
        if mask is not None:
            total = jnp.where(mask, total, 0.0)
        out_ref[pl.ds(at, W), :] = total
        return carry

    lax.fori_loop(0, W, one, 0, unroll=4)


def weigh(rows, vector):
    total = rows[0] * vector[0:1, :]
    for k in range(1, W):
        total = total + rows[k] * vector[k : k + 1, :]
    return total


def kernel(
    T,
    obs_ref,
    pres_ref,
    load_ref,
    nv_ref,
    rb_ref,
    trans_ref,
    innov_ref,
    pmean_ref,
    pvar_ref,
    fm_ref,
    sm_ref,
    sv_ref,
    acc,
    stage,
    recv,
    stage2,
    recv2,
    jm,
    km,
    ym,
    bm,
    nm,
    gm,
    em,
    j1,
    k1,
    const,
    info,
    send_sem,
    recv_sem,
    send_sem2,
    recv_sem2,
):
    per = LANES // T
    me = lax.axis_index("tm")
    barrier = pltpu.get_barrier_semaphore()

    def greet(k, c):
        pl.semaphore_signal(
            barrier, inc=1, device_id={"tm": lax.rem(me + k, T)}, device_id_type=MESH
        )
        return c

    lax.fori_loop(1, T, greet, 0)

    total = obs_ref.shape[1]
    row_at = lax.broadcasted_iota(jnp.int32, (LANES, CHUNK), 0)
    block_of = (row_at % T) * per + row_at // T

    def portion(step, c):
        at = pl.ds(pl.multiple_of(step * CHUNK, CHUNK), CHUNK)
        weight = pres_ref[:, at].astype(jnp.float32) / nv_ref[:, at]
        load = load_ref[:, at]
        lw = load * weight
        parts = [lw * load]
        for d in range(1, W // 2 + 1):
            parts.append(lw * pltpu.roll(load, W - d, 0))
        parts.append(lw * obs_ref[:, at])
        high = [p.astype(jnp.bfloat16) for p in parts]
        low = [(p - h.astype(jnp.float32)).astype(jnp.bfloat16) for p, h in zip(parts, high)]
        fill = [jnp.zeros((2 * LANES - W * len(parts), CHUNK), jnp.bfloat16)]
        onehot = (rb_ref[:, at] == block_of).astype(jnp.float32).astype(jnp.bfloat16)
        dims = (((1,), (1,)), ((), ()))
        got = lax.dot_general(
            onehot,
            jnp.concatenate(high + fill, axis=0),
            dims,
            preferred_element_type=jnp.float32,
        ) + lax.dot_general(
            onehot,
            jnp.concatenate(low + fill, axis=0),
            dims,
            preferred_element_type=jnp.float32,
        )

        @pl.when(step == 0)
        def _():
            acc[...] = got

        @pl.when(step > 0)
        def _():
            acc[...] += got

        return c

    lax.fori_loop(0, total // CHUNK, portion, 0)
    if per < 8:
        stage[...] = jnp.zeros_like(stage)
        stage2[...] = jnp.zeros_like(stage2)
    for h in range(2):
        for b in range(per):
            stage[h, pl.ds(b, T, stride=8), :] = acc[
                b * T : (b + 1) * T, h * LANES : (h + 1) * LANES
            ]

    pl.semaphore_wait(barrier, T - 1)

    def first(k):
        peer = lax.rem(me + k, T)
        return pltpu.make_async_remote_copy(
            src_ref=stage.at[:, pl.ds(pl.multiple_of(peer * 8, 8), 8), :],
            dst_ref=recv.at[:, pl.ds(pl.multiple_of(me * 8, 8), 8), :],
            send_sem=send_sem.at[k],
            recv_sem=recv_sem.at[k],
            device_id={"tm": peer},
            device_id_type=MESH,
        )

    def second(k):
        peer = lax.rem(me + k, T)
        return pltpu.make_async_remote_copy(
            src_ref=stage2.at[pl.ds(pl.multiple_of(peer * 8, 8), 8), :],
            dst_ref=recv2.at[pl.ds(pl.multiple_of(me * 8, 8), 8), :],
            send_sem=send_sem2.at[k],
            recv_sem=recv_sem2.at[k],
            device_id={"tm": peer},
            device_id_type=MESH,
        )

    def begin(make):
        def one(k, c):
            make(k).start()
            return c

        lax.fori_loop(1, T, one, 0)

    def finish(make):
        def one(k, c):
            make(k).wait()
            return c

        lax.fori_loop(1, T, one, 0)

    begin(first)
    mine = pl.ds(pl.multiple_of(me * 8, 8), 8)
    recv[:, mine, :] = stage[:, mine, :]

    lane_from = lax.broadcasted_iota(jnp.int32, (LANES, LANES), 0)
    lane_to = lax.broadcasted_iota(jnp.int32, (LANES, LANES), 1)
    pick = (lane_from == me * per + lane_to // T).astype(jnp.float32)
    whole = jnp.concatenate(
        [trans_ref[...], innov_ref[...], pmean_ref[...], pvar_ref[...]], axis=0
    )
    const[...] = jnp.dot(
        whole, pick, precision=lax.Precision.HIGHEST, preferred_element_type=jnp.float32
    )
    sub = lax.broadcasted_iota(jnp.int32, (W, LANES), 0)
    hour = lax.broadcasted_iota(jnp.int32, (W, LANES), 1) % T
    opening = hour == 0
    inv_noise = 1.0 / const[W2 : W2 + W, :]
    inv_prior = 1.0 / const[W2 + 2 * W : W2 + 3 * W, :]
    start_mean = const[W2 + W : W2 + 2 * W, :] * inv_prior
    for i in range(W):
        km[i * W : (i + 1) * W, :] = jnp.where(
            opening, 0.0, -const[i * W : (i + 1) * W, :] * inv_noise[i : i + 1, :]
        )
    flipped = [-r for r in load_rows(km)]
    multiply(jm, const, flipped, turned=True)
    bm[...] = jnp.zeros_like(bm)

    finish(first)
    for h in range(2):
        joined = jnp.concatenate(
            [recv[h, pl.ds(b, T, stride=8), :] for b in range(per)], axis=0
        )
        info[h * LANES : (h + 1) * LANES, :] = joined.T
    diag = jnp.where(opening, inv_prior, inv_noise)
    for i in range(W):
        for j in range(W):
            gap = (j - i) % W
            row = gap * W + i if gap <= W // 2 else (W - gap) * W + j
            ym[i * W + j : i * W + j + 1, :] = info[row : row + 1, :]
    for i in range(W):
        ym[i * W : (i + 1) * W, :] += jnp.where(sub == i, diag, 0.0)
    npair = (W // 2 + 1) * W
    yv = info[npair : npair + W, :] + jnp.where(opening, start_mean, 0.0)
    ev = jnp.zeros((W, LANES), jnp.float32)
    bv = jnp.zeros((W, LANES), jnp.float32)

    rounds = (T - 1).bit_length()

    def doubling(step, carry):
        yv, ev, bv = carry
        s = jnp.left_shift(1, step)
        keep = hour + s <= T - 1
        rows = negative_inverse(
            [ym[i * W : (i + 1) * W, :] + bm[i * W : (i + 1) * W, :] for i in range(W)]
        )
        store_rows(nm, rows)
        drive = weigh(rows, yv + bv)
        krows = load_rows(km)
        xv = ev + weigh(krows, drive)
        multiply(gm, nm, krows)
        multiply(em, km, load_rows(gm), turned=True, start=jm)
        for i in range(W):
            at = slice(i * W, (i + 1) * W)
            bm[at, :] = jnp.where(keep, pltpu.roll(em[at, :], LANES - s, 1), bm[at, :])
        bv = jnp.where(keep, pltpu.roll(xv, LANES - s, 1), bv)
        inside = hour >= s
        for i in range(W):
            at = slice(i * W, (i + 1) * W)
            k1[at, :] = pltpu.roll(km[at, :], s, 1)
            j1[at, :] = pltpu.roll(jm[at, :], s, 1)
        rows = negative_inverse(
            [
                pltpu.roll(ym[i * W : (i + 1) * W, :], s, 1) + jm[i * W : (i + 1) * W, :]
                for i in range(W)
            ]
        )
        store_rows(nm, rows)
        drive = weigh(rows, pltpu.roll(yv, s, 1) + ev)
        columns = load_columns(km)
        yv = yv + weigh(columns, drive)
        multiply(em, nm, columns)
        multiply(ym, km, load_rows(em), start=ym)
        k1rows = load_rows(k1)
        ev = jnp.where(inside, pltpu.roll(ev, s, 1) + weigh(k1rows, drive), 0.0)
        multiply(gm, nm, k1rows)
        grows = load_rows(gm)
        multiply(jm, k1, grows, turned=True, start=j1, mask=inside)
        multiply(em, km, grows)
        km[...] = em[...]
        return yv, ev, bv

    yv, ev, bv = lax.fori_loop(0, rounds, doubling, (yv, ev, bv))

    rows = negative_inverse(load_rows(ym))
    em[0:W, :] = -weigh(rows, yv)
    rows = negative_inverse(
        [ym[i * W : (i + 1) * W, :] + bm[i * W : (i + 1) * W, :] for i in range(W)]
    )
    em[W : 2 * W, :] = -weigh(rows, yv + bv)
    spread = jnp.where(sub == 0, rows[0], 0.0)
    for i in range(1, W):
        spread = spread + jnp.where(sub == i, rows[i], 0.0)
    em[2 * W : 3 * W, :] = -spread
    em[3 * W : 8 * W, :] = jnp.zeros((5 * W, LANES), jnp.float32)
    gm[0:LANES, :] = em[0:LANES, :].T
    for b in range(per):
        stage2[pl.ds(b, T, stride=8), :] = gm[b * T : (b + 1) * T, :]
    begin(second)
    recv2[mine, :] = stage2[mine, :]
    finish(second)
    if per == 8:
        em[0:LANES, :] = recv2[...].T
    else:
        at_row = lax.broadcasted_iota(jnp.int32, (LANES, 8 * T), 0)
        at_col = lax.broadcasted_iota(jnp.int32, (LANES, 8 * T), 1)
        order = (at_col == (at_row // per) * 8 + at_row % per).astype(jnp.float32)
        em[0:LANES, :] = jnp.dot(
            order,
            recv2[...],
            precision=lax.Precision.HIGHEST,
            preferred_element_type=jnp.float32,
        ).T
    for o, ref in enumerate((fm_ref, sm_ref, sv_ref)):
        for i in range(W):
            ref[0:1, i * LANES : (i + 1) * LANES] = em[o * W + i : o * W + i + 1, :]


def body(T, observed, present, loading, noise_var, region_block, transition, innovation, pmean, pvar):
    regions = observed.shape[1]
    extra = -regions % CHUNK
    padded = regions + extra
    wide = ((0, 0), (0, extra))
    f32 = jnp.float32
    mat = pltpu.VMEM((W2, LANES), f32)
    vmem = pl.BlockSpec(memory_space=pltpu.VMEM)
    out = jax.ShapeDtypeStruct((1, W * LANES), f32)
    return pl.pallas_call(
        functools.partial(kernel, T),
        out_shape=(out, out, out),
        in_specs=[vmem] * 9,
        out_specs=(vmem, vmem, vmem),
        scratch_shapes=[
            pltpu.VMEM((LANES, 2 * LANES), f32),
            pltpu.VMEM((2, 8 * T, LANES), f32),
            pltpu.VMEM((2, 8 * T, LANES), f32),
            pltpu.VMEM((8 * T, LANES), f32),
            pltpu.VMEM((8 * T, LANES), f32),
            mat,
            mat,
            mat,
            mat,
            mat,
            mat,
            mat,
            mat,
            mat,
            pltpu.VMEM((W2 + 3 * W, LANES), f32),
            mat,
            pltpu.SemaphoreType.DMA((T,)),
            pltpu.SemaphoreType.DMA((T,)),
            pltpu.SemaphoreType.DMA((T,)),
            pltpu.SemaphoreType.DMA((T,)),
        ],
        compiler_params=pltpu.CompilerParams(
            collective_id=0, has_side_effects=True, vmem_limit_bytes=32 * 1024 * 1024
        ),
    )(
        jnp.pad(observed, wide),
        jnp.pad(present, wide),
        jnp.pad(loading.T, wide),
        jnp.pad(noise_var[None], wide, constant_values=1.0),
        jnp.pad(region_block[None], wide, constant_values=-1),
        transition.reshape(W2, LANES),
        innovation.reshape(W, LANES),
        pmean.reshape(W, LANES),
        pvar.reshape(W, LANES),
    )


def solution(mesh):
    T = mesh.shape["tm"]
    return jax.shard_map(
        functools.partial(body, T),
        mesh=mesh,
        in_specs=(
            P(("ens", "tm"), None),
            P(("ens", "tm"), None),
            P(),
            P(),
            P(),
            P(),
            P(),
            P(),
            P(),
        ),
        out_specs=(P(("ens", "tm"), None), P(("ens", "tm"), None), P(("ens", "tm"), None)),
        check_vma=False,
    )
```

profile of v0, /device:TPU:0, one launch (start us, length us, event | category | flops | bytes accessed | tf_op | source)
XLA Modules:
  0.0 31.1 jit_solution(9166506305028591778)
XLA Ops:
  0.6 0.0 copy-start.4
  0.6 0.7 %copy-done.4 = f32[1,3000]{1,0:T(1,128)S(1)} copy-done((f32[1,3000]{1,0:T(1,128)S(1)}, f32[1,3000]{1,0:T(1,128)}, u32[]{:S(2)}) %copy-start.4) | copy-done | bytes 12024
  1.3 0.0 copy-start.5
  1.4 0.7 %copy-done.5 = s32[1,3000]{1,0:T(1,128)S(1)} copy-done((s32[1,3000]{1,0:T(1,128)S(1)}, s32[1,3000]{1,0:T(1,128)}, u32[]{:S(2)}) %copy-start.5) | copy-done | bytes 12024
  2.0 0.0 copy-start.6
  2.1 0.7 %copy-done.6 = f32[3000]{0:T(1024)S(1)} copy-done((f32[3000]{0:T(1024)S(1)}, f32[3000]{0:T(1024)}, u32[]{:S(2)}) %copy-start.6) | copy-done | bytes 12024
  2.8 0.0 copy-start.7
  2.8 0.7 %copy-done.7 = s32[3000]{0:T(1024)S(1)} copy-done((s32[3000]{0:T(1024)S(1)}, s32[3000]{0:T(1024)}, u32[]{:S(2)}) %copy-start.7) | copy-done | bytes 12024
  3.5 0.0 copy-start
  3.5 0.0 copy-start.1
  3.5 0.0 copy-start.2
  3.5 0.0 copy-start.3
  3.5 1.0 %pad.21.load_ref = f32[16,3072]{1,0:T(8,128)S(1)} pad(f32[16,3000]{1,0:T(8,128)} %bitcast.11, f32[]{:T(128)} %constant.1.clone.1), padding=0_0x0_72 | pad | bytes 388612 | tf_op jit(solution)/shard_map/jit(_pad)/pad | solution.py:374
  4.5 0.0 copy-done
  4.5 0.0 copy-done.1
  4.5 0.0 copy-done.2
  4.6 0.0 copy-done.3
  4.6 24.7 %shard_map.112 = (f32[1,2048]{1,0:T(1,128)S(1)}, f32[1,2048]{1,0:T(1,128)S(1)}, f32[1,2048]{1,0:T(1,128)S(1)}) custom-call(f32[1,3072]{1,0:T(1,128)S(1)} %pad.19.obs_ref, s32[1,3072]{1,0:T(1,128)S(1)} %pad.20.pres_ref, f32[16,3072]{1,0:T(8,128)S(1)} %pad.21.load_ref, f32[1,3072]{1,0:T(1,128)S(1)} %pad.22.nv_ref, s32[1,3072]{1,0:T(1,128)S(1)} %pad.23.rb_ref, ...), custom_call_target="tpu_custom_call" | custom-call | tf_op jit(solution)/shard_map/pallas_call | solution.py:341
  29.3 0.6 %copy.15 = f32[1,2048]{1,0:T(1,128)} copy(f32[1,2048]{1,0:T(1,128)S(1)} %get-tuple-element.6) | data formatting | bytes 16384
  29.9 0.6 %copy.16 = f32[1,2048]{1,0:T(1,128)} copy(f32[1,2048]{1,0:T(1,128)S(1)} %get-tuple-element.7) | data formatting | bytes 16384
  30.5 0.6 %copy.17 = f32[1,2048]{1,0:T(1,128)} copy(f32[1,2048]{1,0:T(1,128)S(1)} %get-tuple-element.8) | data formatting | bytes 16384
  (4 shorter events, 0.0 us)
Async XLA Ops:
  0.6 0.7 %copy-start.4 = (f32[1,3000]{1,0:T(1,128)S(1)}, f32[1,3000]{1,0:T(1,128)}, u32[]{:S(2)}) copy-start(f32[1,3000]{1,0:T(1,128)} %param.9) | copy-start | bytes 36004
  1.3 0.7 %copy-start.5 = (s32[1,3000]{1,0:T(1,128)S(1)}, s32[1,3000]{1,0:T(1,128)}, u32[]{:S(2)}) copy-start(s32[1,3000]{1,0:T(1,128)} %param.10) | copy-start | bytes 36004
  2.0 0.7 %copy-start.6 = (f32[3000]{0:T(1024)S(1)}, f32[3000]{0:T(1024)}, u32[]{:S(2)}) copy-start(f32[3000]{0:T(1024)} %param.12) | copy-start | bytes 36004
  2.8 0.7 %copy-start.7 = (s32[3000]{0:T(1024)S(1)}, s32[3000]{0:T(1024)}, u32[]{:S(2)}) copy-start(s32[3000]{0:T(1024)} %param.13) | copy-start | bytes 36004
  3.5 1.1 %copy-start = (f32[16,16,128]{2,1,0:T(8,128)S(1)}, f32[16,16,128]{2,1,0:T(8,128)}, u32[]{:S(2)}) copy-start(f32[16,16,128]{2,1,0:T(8,128)} %param.14) | copy-start | bytes 393220
  3.5 1.1 %copy-start.1 = (f32[2048]{0:T(1024)S(1)}, f32[2048]{0:T(1024)}, u32[]{:S(2)}) copy-start(f32[2048]{0:T(1024)} %param.15) | copy-start | bytes 24580
  3.5 1.1 %copy-start.2 = (f32[2048]{0:T(1024)S(1)}, f32[2048]{0:T(1024)}, u32[]{:S(2)}) copy-start(f32[2048]{0:T(1024)} %param.16) | copy-start | bytes 24580
  3.5 1.1 %copy-start.3 = (f32[2048]{0:T(1024)S(1)}, f32[2048]{0:T(1024)}, u32[]{:S(2)}) copy-start(f32[2048]{0:T(1024)} %param.17) | copy-start | bytes 24580
where the time goes:
time: 31.5 us; the launch traced here: 31.1 us
  Pallas kernels  24.7 us (78%)
  local copies, waits for them, and re-layouts  5.65 us (18%)
  between operations  0.73 us (2%)
    pallas_call x1, Pallas kernels, body(): pl.pallas_call(functools.partial(kernel, T), out_shape=(out, out, out), i...  24.7 us
    unnamed x19, local copies, waits for them, and re-layouts  4.6 us
    pad x1, local copies, waits for them, and re-layouts, body(): jnp.pad(loading.T, wide)  1 us

commit v1 on v0

--- a/solution.py
+++ b/solution.py
@@ -69,19 +69,25 @@
 
 def kernel(
     T,
+    obs_hbm,
+    pres_hbm,
+    load_hbm,
+    nv_hbm,
+    rb_hbm,
+    trans_hbm,
+    innov_hbm,
+    pmean_hbm,
+    pvar_hbm,
+    fm_ref,
+    sm_ref,
+    sv_ref,
     obs_ref,
     pres_ref,
     load_ref,
     nv_ref,
     rb_ref,
-    trans_ref,
-    innov_ref,
-    pmean_ref,
-    pvar_ref,
-    fm_ref,
-    sm_ref,
-    sv_ref,
-    acc,
+    whole,
+    fetch_sem,
     stage,
     recv,
     stage2,
@@ -103,36 +109,56 @@
     recv_sem2,
 ):
     per = LANES // T
+    regions = obs_hbm.shape[1]
     me = lax.axis_index("tm")
     barrier = pltpu.get_barrier_semaphore()
 
-    def greet(k, c):
+    fetches = [
+        pltpu.make_async_copy(src, dst, fetch_sem.at[n])
+        for n, (src, dst) in enumerate(
+            (
+                (pres_hbm, pres_ref),
+                (nv_hbm, nv_ref),
+                (load_hbm, load_ref),
+                (obs_hbm, obs_ref),
+                (rb_hbm, rb_ref),
+                (trans_hbm, whole.at[pl.ds(0, W2), :]),
+                (innov_hbm, whole.at[pl.ds(W2, W), :]),
+                (pmean_hbm, whole.at[pl.ds(W2 + W, W), :]),
+                (pvar_hbm, whole.at[pl.ds(W2 + 2 * W, W), :]),
+            )
+        )
+    ]
+    for f in fetches:
+        f.start()
+    for k in range(1, T):
         pl.semaphore_signal(
             barrier, inc=1, device_id={"tm": lax.rem(me + k, T)}, device_id_type=MESH
         )
-        return c
-
-    lax.fori_loop(1, T, greet, 0)
-
-    total = obs_ref.shape[1]
-    row_at = lax.broadcasted_iota(jnp.int32, (LANES, CHUNK), 0)
+    for f in fetches[:5]:
+        f.wait()
+
+    row_at = lax.broadcasted_iota(jnp.int32, (LANES, 1), 0)
     block_of = (row_at % T) * per + row_at // T
 
-    def portion(step, c):
-        at = pl.ds(pl.multiple_of(step * CHUNK, CHUNK), CHUNK)
+    got = None
+    for low_end in range(0, regions, CHUNK):
+        wide = min(CHUNK, regions - low_end)
+        at = slice(low_end, low_end + wide)
         weight = pres_ref[:, at].astype(jnp.float32) / nv_ref[:, at]
         load = load_ref[:, at]
+        value = obs_ref[:, at]
         lw = load * weight
         parts = [lw * load]
         for d in range(1, W // 2 + 1):
             parts.append(lw * pltpu.roll(load, W - d, 0))
-        parts.append(lw * obs_ref[:, at])
+        parts.append(lw * value)
         high = [p.astype(jnp.bfloat16) for p in parts]
         low = [(p - h.astype(jnp.float32)).astype(jnp.bfloat16) for p, h in zip(parts, high)]
-        fill = [jnp.zeros((2 * LANES - W * len(parts), CHUNK), jnp.bfloat16)]
+        fill = [jnp.zeros((2 * LANES - W * len(parts), wide), jnp.bfloat16)]
         onehot = (rb_ref[:, at] == block_of).astype(jnp.float32).astype(jnp.bfloat16)
         dims = (((1,), (1,)), ((), ()))
-        got = lax.dot_general(
+        new = lax.dot_general(
             onehot,
             jnp.concatenate(high + fill, axis=0),
             dims,
@@ -144,76 +170,23 @@
             preferred_element_type=jnp.float32,
         )
 
-        @pl.when(step == 0)
-        def _():
-            acc[...] = got
-
-        @pl.when(step > 0)
-        def _():
-            acc[...] += got
-
-        return c
-
-    lax.fori_loop(0, total // CHUNK, portion, 0)
+        got = new if got is None else got + new
     if per < 8:
         stage[...] = jnp.zeros_like(stage)
         stage2[...] = jnp.zeros_like(stage2)
     for h in range(2):
         for b in range(per):
-            stage[h, pl.ds(b, T, stride=8), :] = acc[
+            stage[h, pl.ds(b, T, stride=8), :] = got[
                 b * T : (b + 1) * T, h * LANES : (h + 1) * LANES
             ]
-
-    pl.semaphore_wait(barrier, T - 1)
-
-    def first(k):
-        peer = lax.rem(me + k, T)
-        return pltpu.make_async_remote_copy(
-            src_ref=stage.at[:, pl.ds(pl.multiple_of(peer * 8, 8), 8), :],
-            dst_ref=recv.at[:, pl.ds(pl.multiple_of(me * 8, 8), 8), :],
-            send_sem=send_sem.at[k],
-            recv_sem=recv_sem.at[k],
-            device_id={"tm": peer},
-            device_id_type=MESH,
-        )
-
-    def second(k):
-        peer = lax.rem(me + k, T)
-        return pltpu.make_async_remote_copy(
-            src_ref=stage2.at[pl.ds(pl.multiple_of(peer * 8, 8), 8), :],
-            dst_ref=recv2.at[pl.ds(pl.multiple_of(me * 8, 8), 8), :],
-            send_sem=send_sem2.at[k],
-            recv_sem=recv_sem2.at[k],
-            device_id={"tm": peer},
-            device_id_type=MESH,
-        )
-
-    def begin(make):
-        def one(k, c):
-            make(k).start()
-            return c
-
-        lax.fori_loop(1, T, one, 0)
-
-    def finish(make):
-        def one(k, c):
-            make(k).wait()
-            return c
-
-        lax.fori_loop(1, T, one, 0)
-
-    begin(first)
-    mine = pl.ds(pl.multiple_of(me * 8, 8), 8)
-    recv[:, mine, :] = stage[:, mine, :]
 
     lane_from = lax.broadcasted_iota(jnp.int32, (LANES, LANES), 0)
     lane_to = lax.broadcasted_iota(jnp.int32, (LANES, LANES), 1)
     pick = (lane_from == me * per + lane_to // T).astype(jnp.float32)
-    whole = jnp.concatenate(
-        [trans_ref[...], innov_ref[...], pmean_ref[...], pvar_ref[...]], axis=0
-    )
+    for f in fetches[5:]:
+        f.wait()
     const[...] = jnp.dot(
-        whole, pick, precision=lax.Precision.HIGHEST, preferred_element_type=jnp.float32
+        whole[...], pick, precision=lax.Precision.HIGHEST, preferred_element_type=jnp.float32
     )
     sub = lax.broadcasted_iota(jnp.int32, (W, LANES), 0)
     hour = lax.broadcasted_iota(jnp.int32, (W, LANES), 1) % T
@@ -229,7 +202,40 @@
     multiply(jm, const, flipped, turned=True)
     bm[...] = jnp.zeros_like(bm)
 
-    finish(first)
+    pl.semaphore_wait(barrier, T - 1)
+
+    def first(k):
+        peer = lax.rem(me + k, T)
+        return pltpu.make_async_remote_copy(
+            src_ref=stage.at[:, pl.ds(pl.multiple_of(peer * 8, 8), 8), :],
+            dst_ref=recv.at[:, pl.ds(pl.multiple_of(me * 8, 8), 8), :],
+            send_sem=send_sem,
+            recv_sem=recv_sem,
+            device_id={"tm": peer},
+            device_id_type=MESH,
+        )
+
+    def second(k):
+        peer = lax.rem(me + k, T)
+        return pltpu.make_async_remote_copy(
+            src_ref=stage2.at[pl.ds(pl.multiple_of(peer * 8, 8), 8), :],
+            dst_ref=recv2.at[pl.ds(pl.multiple_of(me * 8, 8), 8), :],
+            send_sem=send_sem2,
+            recv_sem=recv_sem2,
+            device_id={"tm": peer},
+            device_id_type=MESH,
+        )
+
+    def begin(make):
+        for k in range(1, T):
+            make(k).start()
+
+    begin(first)
+    mine = pl.ds(pl.multiple_of(me * 8, 8), 8)
+    recv[:, mine, :] = stage[:, mine, :]
+
+    rest = pl.ds(0, (T - 1) * 8)
+    pltpu.make_async_copy(recv.at[:, rest, :], recv.at[:, rest, :], recv_sem).wait()
     for h in range(2):
         joined = jnp.concatenate(
             [recv[h, pl.ds(b, T, stride=8), :] for b in range(per)], axis=0
@@ -311,7 +317,7 @@
         stage2[pl.ds(b, T, stride=8), :] = gm[b * T : (b + 1) * T, :]
     begin(second)
     recv2[mine, :] = stage2[mine, :]
-    finish(second)
+    pltpu.make_async_copy(recv2.at[rest, :], recv2.at[rest, :], recv_sem2).wait()
     if per == 8:
         em[0:LANES, :] = recv2[...].T
     else:
@@ -327,13 +333,12 @@
     for o, ref in enumerate((fm_ref, sm_ref, sv_ref)):
         for i in range(W):
             ref[0:1, i * LANES : (i + 1) * LANES] = em[o * W + i : o * W + i + 1, :]
+    pltpu.make_async_copy(stage.at[:, rest, :], stage.at[:, rest, :], send_sem).wait()
+    pltpu.make_async_copy(stage2.at[rest, :], stage2.at[rest, :], send_sem2).wait()
 
 
 def body(T, observed, present, loading, noise_var, region_block, transition, innovation, pmean, pvar):
     regions = observed.shape[1]
-    extra = -regions % CHUNK
-    padded = regions + extra
-    wide = ((0, 0), (0, extra))
     f32 = jnp.float32
     mat = pltpu.VMEM((W2, LANES), f32)
     vmem = pl.BlockSpec(memory_space=pltpu.VMEM)
@@ -341,10 +346,16 @@
     return pl.pallas_call(
         functools.partial(kernel, T),
         out_shape=(out, out, out),
-        in_specs=[vmem] * 9,
+        in_specs=[pl.BlockSpec(memory_space=pl.ANY)] * 9,
         out_specs=(vmem, vmem, vmem),
         scratch_shapes=[
-            pltpu.VMEM((LANES, 2 * LANES), f32),
+            pltpu.VMEM((1, regions), f32),
+            pltpu.VMEM((1, regions), jnp.int32),
+            pltpu.VMEM((W, regions), f32),
+            pltpu.VMEM((1, regions), f32),
+            pltpu.VMEM((1, regions), jnp.int32),
+            pltpu.VMEM((W2 + 3 * W, LANES), f32),
+            pltpu.SemaphoreType.DMA((9,)),
             pltpu.VMEM((2, 8 * T, LANES), f32),
             pltpu.VMEM((2, 8 * T, LANES), f32),
             pltpu.VMEM((8 * T, LANES), f32),
@@ -360,20 +371,20 @@
             mat,
             pltpu.VMEM((W2 + 3 * W, LANES), f32),
             mat,
-            pltpu.SemaphoreType.DMA((T,)),
-            pltpu.SemaphoreType.DMA((T,)),
-            pltpu.SemaphoreType.DMA((T,)),
-            pltpu.SemaphoreType.DMA((T,)),
+            pltpu.SemaphoreType.DMA,
+            pltpu.SemaphoreType.DMA,
+            pltpu.SemaphoreType.DMA,
+            pltpu.SemaphoreType.DMA,
         ],
         compiler_params=pltpu.CompilerParams(
             collective_id=0, has_side_effects=True, vmem_limit_bytes=32 * 1024 * 1024
         ),
     )(
-        jnp.pad(observed, wide),
-        jnp.pad(present, wide),
-        jnp.pad(loading.T, wide),
-        jnp.pad(noise_var[None], wide, constant_values=1.0),
-        jnp.pad(region_block[None], wide, constant_values=-1),
+        observed,
+        present,
+        loading.T,
+        noise_var[None],
+        region_block[None],
         transition.reshape(W2, LANES),
         innovation.reshape(W, LANES),
         pmean.reshape(W, LANES),

time: 31.5 us -> 34.6 us (1.098)
  local copies, waits for them, and re-layouts: 5.65 us -> 8.53 us
    unnamed x19 -> x21, local copies, waits for them, and re-layouts: 4.6 us -> 8.53 us
    pad x5 -> x0, local copies, waits for them, and re-layouts: 1.05 us -> none  [the longest x1 1 us: body(): jnp.pad(loading.T, wide)]
where the time goes in v1:
time: 34.6 us; the launch traced here: 34 us
  Pallas kernels  24.8 us (72%)
  local copies, waits for them, and re-layouts  8.53 us (25%)
  between operations  0.66 us (2%)
    pallas_call x1, Pallas kernels, body(): pl.pallas_call(functools.partial(kernel, T), out_shape=(out, out, out), i...  24.8 us
    unnamed x21, local copies, waits for them, and re-layouts  8.53 us

profile of v1, /device:TPU:0, one launch (start us, length us, event | category | flops | bytes accessed | tf_op | source)
XLA Modules:
  0.0 34.0 jit_solution(12523646607904189824)
XLA Ops:
  0.6 0.0 copy-start.2
  0.6 0.7 %copy-done.2 = f32[1,3000]{1,0:T(1,128)S(1)} copy-done((f32[1,3000]{1,0:T(1,128)S(1)}, f32[1,3000]{1,0:T(1,128)}, u32[]{:S(2)}) %copy-start.2) | copy-done | bytes 12024
  1.3 0.0 copy-start
  1.3 0.9 %copy-done = f32[3000,16]{0,1:T(8,128)S(1)} copy-done((f32[3000,16]{0,1:T(8,128)S(1)}, f32[3000,16]{0,1:T(8,128)}, u32[]{:S(2)}) %copy-start) | copy-done | bytes 192024
  2.3 0.0 copy-start.1
  2.3 0.9 %copy-done.1 = f32[16,16,128]{2,1,0:T(8,128)S(1)} copy-done((f32[16,16,128]{2,1,0:T(8,128)S(1)}, f32[16,16,128]{2,1,0:T(8,128)}, u32[]{:S(2)}) %copy-start.1) | copy-done | bytes 131096
  3.2 0.0 copy-start.3
  3.2 0.7 %copy-done.3 = s32[1,3000]{1,0:T(1,128)S(1)} copy-done((s32[1,3000]{1,0:T(1,128)S(1)}, s32[1,3000]{1,0:T(1,128)}, u32[]{:S(2)}) %copy-start.3) | copy-done | bytes 12024
  3.9 0.0 copy-start.4
  3.9 0.7 %copy-done.4 = f32[3000]{0:T(1024)S(1)} copy-done((f32[3000]{0:T(1024)S(1)}, f32[3000]{0:T(1024)}, u32[]{:S(2)}) %copy-start.4) | copy-done | bytes 12024
  4.6 0.0 copy-start.5
  4.6 0.7 %copy-done.5 = s32[3000]{0:T(1024)S(1)} copy-done((s32[3000]{0:T(1024)S(1)}, s32[3000]{0:T(1024)}, u32[]{:S(2)}) %copy-start.5) | copy-done | bytes 12024
  5.3 0.0 copy-start.6
  5.3 0.7 %copy-done.6 = f32[2048]{0:T(1024)S(1)} copy-done((f32[2048]{0:T(1024)S(1)}, f32[2048]{0:T(1024)}, u32[]{:S(2)}) %copy-start.6) | copy-done | bytes 8216
  6.0 0.0 copy-start.7
  6.0 0.7 %copy-done.7 = f32[2048]{0:T(1024)S(1)} copy-done((f32[2048]{0:T(1024)S(1)}, f32[2048]{0:T(1024)}, u32[]{:S(2)}) %copy-start.7) | copy-done | bytes 8216
  6.7 0.0 copy-start.8
  6.7 0.7 %copy-done.8 = f32[2048]{0:T(1024)S(1)} copy-done((f32[2048]{0:T(1024)S(1)}, f32[2048]{0:T(1024)}, u32[]{:S(2)}) %copy-start.8) | copy-done | bytes 8216
  7.4 24.8 %shard_map.112 = (f32[1,2048]{1,0:T(1,128)S(1)}, f32[1,2048]{1,0:T(1,128)S(1)}, f32[1,2048]{1,0:T(1,128)S(1)}) custom-call(f32[1,3000]{1,0:T(1,128)S(1)} %copy-done.2, s32[1,3000]{1,0:T(1,128)S(1)} %copy-done.3, f32[16,3000]{1,0:T(8,128)S(1)} %bitcast.7, f32[1,3000]{1,0:T(1,128)S(1)} %bitcast.9, s32[1,3000]{1,0:T(1,128)S(1)} %bitcast.10, ...), custom_call_target="tpu_custom_call" | custom-call | tf_op jit(solution)/shard_map/pallas_call | solution.py:346
  32.2 0.6 %copy.15 = f32[1,2048]{1,0:T(1,128)} copy(f32[1,2048]{1,0:T(1,128)S(1)} %get-tuple-element.6) | data formatting | bytes 16384
  32.8 0.6 %copy.16 = f32[1,2048]{1,0:T(1,128)} copy(f32[1,2048]{1,0:T(1,128)S(1)} %get-tuple-element.7) | data formatting | bytes 16384
  33.4 0.6 %copy.17 = f32[1,2048]{1,0:T(1,128)} copy(f32[1,2048]{1,0:T(1,128)S(1)} %get-tuple-element.8) | data formatting | bytes 16384
Async XLA Ops:
  0.6 0.7 %copy-start.2 = (f32[1,3000]{1,0:T(1,128)S(1)}, f32[1,3000]{1,0:T(1,128)}, u32[]{:S(2)}) copy-start(f32[1,3000]{1,0:T(1,128)} %obs_hbm.1) | copy-start | bytes 36004
  1.3 0.9 %copy-start = (f32[3000,16]{0,1:T(8,128)S(1)}, f32[3000,16]{0,1:T(8,128)}, u32[]{:S(2)}) copy-start(f32[3000,16]{0,1:T(8,128)} %param.11) | copy-start | bytes 576004
  2.3 0.9 %copy-start.1 = (f32[16,16,128]{2,1,0:T(8,128)S(1)}, f32[16,16,128]{2,1,0:T(8,128)}, u32[]{:S(2)}) copy-start(f32[16,16,128]{2,1,0:T(8,128)} %param.14) | copy-start | bytes 393220
  3.2 0.7 %copy-start.3 = (s32[1,3000]{1,0:T(1,128)S(1)}, s32[1,3000]{1,0:T(1,128)}, u32[]{:S(2)}) copy-start(s32[1,3000]{1,0:T(1,128)} %pres_hbm.1) | copy-start | bytes 36004
  3.9 0.7 %copy-start.4 = (f32[3000]{0:T(1024)S(1)}, f32[3000]{0:T(1024)}, u32[]{:S(2)}) copy-start(f32[3000]{0:T(1024)} %param.12) | copy-start | bytes 36004
  4.6 0.7 %copy-start.5 = (s32[3000]{0:T(1024)S(1)}, s32[3000]{0:T(1024)}, u32[]{:S(2)}) copy-start(s32[3000]{0:T(1024)} %param.13) | copy-start | bytes 36004
  5.3 0.7 %copy-start.6 = (f32[2048]{0:T(1024)S(1)}, f32[2048]{0:T(1024)}, u32[]{:S(2)}) copy-start(f32[2048]{0:T(1024)} %param.15) | copy-start | bytes 24580
  6.0 0.7 %copy-start.7 = (f32[2048]{0:T(1024)S(1)}, f32[2048]{0:T(1024)}, u32[]{:S(2)}) copy-start(f32[2048]{0:T(1024)} %param.16) | copy-start | bytes 24580
  6.7 0.7 %copy-start.8 = (f32[2048]{0:T(1024)S(1)}, f32[2048]{0:T(1024)}, u32[]{:S(2)}) copy-start(f32[2048]{0:T(1024)} %param.17) | copy-start | bytes 24580

commit v2 on v1

--- a/solution.py
+++ b/solution.py
@@ -78,9 +78,7 @@
     innov_hbm,
     pmean_hbm,
     pvar_hbm,
-    fm_ref,
-    sm_ref,
-    sv_ref,
+    out_ref,
     obs_ref,
     pres_ref,
     load_ref,
@@ -318,23 +316,28 @@
     begin(second)
     recv2[mine, :] = stage2[mine, :]
     pltpu.make_async_copy(recv2.at[rest, :], recv2.at[rest, :], recv_sem2).wait()
+    out_ref[...] = recv2[...]
+    pltpu.make_async_copy(stage.at[:, rest, :], stage.at[:, rest, :], send_sem).wait()
+    pltpu.make_async_copy(stage2.at[rest, :], stage2.at[rest, :], send_sem2).wait()
+
+
+def arrange(T, got_ref, fm_ref, sm_ref, sv_ref):
+    per = LANES // T
     if per == 8:
-        em[0:LANES, :] = recv2[...].T
+        full = got_ref[...].T
     else:
         at_row = lax.broadcasted_iota(jnp.int32, (LANES, 8 * T), 0)
         at_col = lax.broadcasted_iota(jnp.int32, (LANES, 8 * T), 1)
         order = (at_col == (at_row // per) * 8 + at_row % per).astype(jnp.float32)
-        em[0:LANES, :] = jnp.dot(
+        full = jnp.dot(
             order,
-            recv2[...],
+            got_ref[...],
             precision=lax.Precision.HIGHEST,
             preferred_element_type=jnp.float32,
         ).T
     for o, ref in enumerate((fm_ref, sm_ref, sv_ref)):
         for i in range(W):
-            ref[0:1, i * LANES : (i + 1) * LANES] = em[o * W + i : o * W + i + 1, :]
-    pltpu.make_async_copy(stage.at[:, rest, :], stage.at[:, rest, :], send_sem).wait()
-    pltpu.make_async_copy(stage2.at[rest, :], stage2.at[rest, :], send_sem2).wait()
+            ref[0:1, i * LANES : (i + 1) * LANES] = full[o * W + i : o * W + i + 1, :]
 
 
 def body(T, observed, present, loading, noise_var, region_block, transition, innovation, pmean, pvar):
@@ -343,11 +346,11 @@
     mat = pltpu.VMEM((W2, LANES), f32)
     vmem = pl.BlockSpec(memory_space=pltpu.VMEM)
     out = jax.ShapeDtypeStruct((1, W * LANES), f32)
-    return pl.pallas_call(
+    got = pl.pallas_call(
         functools.partial(kernel, T),
-        out_shape=(out, out, out),
+        out_shape=jax.ShapeDtypeStruct((8 * T, LANES), f32),
         in_specs=[pl.BlockSpec(memory_space=pl.ANY)] * 9,
-        out_specs=(vmem, vmem, vmem),
+        out_specs=vmem,
         scratch_shapes=[
             pltpu.VMEM((1, regions), f32),
             pltpu.VMEM((1, regions), jnp.int32),
@@ -377,7 +380,7 @@
             pltpu.SemaphoreType.DMA,
         ],
         compiler_params=pltpu.CompilerParams(
-            collective_id=0, has_side_effects=True, vmem_limit_bytes=32 * 1024 * 1024
+            collective_id=0, has_side_effects=True, vmem_limit_bytes=63 * 1024 * 1024
         ),
     )(
         observed,
@@ -390,6 +393,12 @@
         pmean.reshape(W, LANES),
         pvar.reshape(W, LANES),
     )
+    return pl.pallas_call(
+        functools.partial(arrange, T),
+        out_shape=(out, out, out),
+        in_specs=[vmem],
+        out_specs=(vmem, vmem, vmem),
+    )(got)
 
 
 def solution(mesh):

time: 34.6 us -> 27.3 us (0.79)
  local copies, waits for them, and re-layouts: 8.53 us -> 0 us
  Pallas kernels: 24.8 us -> 26.4 us
    unnamed x21 -> x0, local copies, waits for them, and re-layouts: 8.53 us -> none
    pallas_call x1 -> x2, Pallas kernels: 24.8 us -> 26.4 us  [the longest x1 24.9 us: body(): pl.pallas_call(functools.partial(kernel, T), out_shape=jax.ShapeDtypeStru...]
where the time goes in v2:
time: 27.3 us; the launch traced here: 27 us
  Pallas kernels  26.4 us (97%)
  between operations  0.64 us (2%)
    pallas_call x1, Pallas kernels, body(): pl.pallas_call(functools.partial(kernel, T), out_shape=jax.ShapeDtypeStru...  24.9 us
    pallas_call x1, Pallas kernels, body(): pl.pallas_call(functools.partial(arrange, T), out_shape=(out, out, out),...  1.52 us

profile of v2, /device:TPU:0, one launch (start us, length us, event | category | flops | bytes accessed | tf_op | source)
XLA Modules:
  0.0 27.0 jit_solution(10898445185834264628)
XLA Ops:
  0.6 24.9 %shard_map.112.got_ref = f32[128,128]{1,0:T(8,128)} custom-call(f32[1,3000]{1,0:T(1,128)} %obs_hbm.1, s32[1,3000]{1,0:T(1,128)} %pres_hbm.1, f32[16,3000]{1,0:T(8,128)} %bitcast.7, f32[1,3000]{1,0:T(1,128)} %bitcast.9, s32[1,3000]{1,0:T(1,128)} %bitcast.10, f32[256,128]{1,0:T(8,128)} %bitcast.8, f32[16,128]{1,0:T(8,128)} %bitcast.11, f32[16,128]{1,0:T(8,128)} %bitcast.12, ...), custom_call_target="tpu_custom_call" | custom-call | tf_op jit(solution)/shard_map/pallas_call | solution.py:349
  25.5 1.5 %shard_map.113 = (f32[1,2048]{1,0:T(1,128)}, f32[1,2048]{1,0:T(1,128)}, f32[1,2048]{1,0:T(1,128)}) custom-call(f32[128,128]{1,0:T(8,128)} %shard_map.112.got_ref), custom_call_target="tpu_custom_call" | custom-call | tf_op jit(solution)/shard_map/pallas_call | solution.py:396
